TPU v7x, 32 devices: a whole 2x2x4 slice. The times are simulated.
32 devices in a mesh: rows: 4 (over y, x), cols: 8 (over z, core).
Axes of the slice: x: 2, y: 2, z: 4, core: 2. Of those that a mesh axis runs over, the one named last changes fastest.
Arguments:
- c_eta: float32 [512, 2048], P('rows', 'cols'), may hold values from -4 to 4
- c_flux: float32 [2, 512, 2048], P(None, 'rows', 'cols'), may hold values from -150 to 150
- c_depth: float32 [512, 2048], P('rows', 'cols'), may hold values from 100 to 4000
- f_bed: float32 [128, 2048], P('rows', 'cols'), may hold values from -3 to 1
- f_depth: float32 [128, 2048], P('rows', 'cols'), may hold values from 0.05 to 3
- f_wet: int32 [128, 2048], P('rows', 'cols'), may hold values 0 or 1
- f_class: int32 [128, 2048], P('rows', 'cols'), may hold values from 0 to 10
- manning: float32 [11], replicated, may hold values from 0.02 to 0.2
- nest_map: int32 [2048], replicated, may hold values from 0 to 1048575, as said below
Outputs:
- c_eta_out: float32 [512, 2048], P('rows', 'cols')
- f_water: float32 [128, 2048], P('rows', 'cols')
- f_flux: float32 [2, 128, 2048], P(None, 'rows', 'cols')
Inputs may be any that keep to these rules, and one draw needn't show every extreme that they name: `nest_map`: entry b is the flat index, row times 2048 plus column, of the coarse cell that drives fine boundary cell b; entries with the same b // 18 are equal; for s = b // 18 the coarse row lies in [(s * 128) % 512, (s * 128) % 512 + 128) and the coarse column is min(s * 18 * 1 + 256 + j, 2047) for some j in 0..128.
All inputs are finite; a program needn't handle non-finite values. No bound on the sum of `f_wet` on one device may be relied on, other than what follows from the above.
Results may differ from a plain program's by a relative error of at most 0.00002.
Values sent between devices are 32-bit elements; how exact they have to be, the bound alone decides.
A program may use at most 64 MiB of HBM per device.

v0:
```python
import jax
import jax.numpy as jnp
from jax import lax
from jax.sharding import PartitionSpec as P

NCLASS = 11
CSTEPS = 2
SUB = 3
FSTEPS = 6
gravity = 9.81
coarse_spacing = 90.0
coarse_tick = 0.25
fine_spacing = 5.0
depth_floor = 0.01
dry_depth = 0.05


def padded_2(block, sides, width):
    for axis, dim in sides:
        count = lax.axis_size(axis)
        forward = [(i, i + 1) for i in range(count - 1)]
        backward = [(target, source) for source, target in forward]
        low = lax.ppermute(
            lax.slice_in_dim(block, block.shape[dim] - width, None, axis=dim), axis, forward
        )
        high = lax.ppermute(lax.slice_in_dim(block, 0, width, axis=dim), axis, backward)
        block = jnp.concatenate([low, block, high], axis=dim)
    return block


def coarse_update(padded):
    surf = padded[0]
    total = padded[1]
    rows_flux = padded[2]
    cols_flux = padded[3]
    face_rows = jnp.minimum(total[:-1, 1:-1], total[1:, 1:-1])
    new_rows = jnp.minimum(face_rows, 1.0) * (
        rows_flux[:-1, 1:-1]
        - coarse_tick * gravity * face_rows * (surf[1:, 1:-1] - surf[:-1, 1:-1]) / coarse_spacing
    )
    face_cols = jnp.minimum(total[1:-1, :-1], total[1:-1, 1:])
    new_cols = jnp.minimum(face_cols, 1.0) * (
        cols_flux[1:-1, :-1]
        - coarse_tick * gravity * face_cols * (surf[1:-1, 1:] - surf[1:-1, :-1]) / coarse_spacing
    )
    surface = surf[1:-1, 1:-1] - coarse_tick / coarse_spacing * (
        new_rows[1:] - new_rows[:-1] + (new_cols[:, 1:] - new_cols[:, :-1])
    )
    return (surface, new_rows[1:], new_cols[:, 1:])


def face_flux(flux_old, face_depth, slope, rough, fine_tick):
    wetness = jnp.minimum(face_depth / dry_depth, 1.0)
    driven = flux_old - fine_tick * gravity * face_depth * slope / fine_spacing
    friction = 1.0 + fine_tick * gravity * rough * rough * jnp.abs(flux_old) / jnp.power(
        jnp.maximum(face_depth, depth_floor), 7.0 / 3.0
    )
    return wetness * driven / friction


def fine_faces(water_pad, bed_pad, rough_pad, rows_pad, cols_pad, fine_tick):
    surf = bed_pad + water_pad
    depth_rows = jnp.maximum(
        jnp.maximum(surf[:-1, 1:-1], surf[1:, 1:-1])
        - jnp.maximum(bed_pad[:-1, 1:-1], bed_pad[1:, 1:-1]),
        0.0,
    )
    rough_rows = 0.5 * (rough_pad[:-1, 1:-1] + rough_pad[1:, 1:-1])
    new_rows = face_flux(
        rows_pad[:-1, 1:-1], depth_rows, surf[1:, 1:-1] - surf[:-1, 1:-1], rough_rows, fine_tick
    )
    depth_cols = jnp.maximum(
        jnp.maximum(surf[1:-1, :-1], surf[1:-1, 1:])
        - jnp.maximum(bed_pad[1:-1, :-1], bed_pad[1:-1, 1:]),
        0.0,
    )
    rough_cols = 0.5 * (rough_pad[1:-1, :-1] + rough_pad[1:-1, 1:])
    new_cols = face_flux(
        cols_pad[1:-1, :-1], depth_cols, surf[1:-1, 1:] - surf[1:-1, :-1], rough_cols, fine_tick
    )
    return (new_rows, new_cols)


def open_boundary(water_top, bed_top, bnd_surface, bnd_velocity):
    return water_top * bnd_velocity + jnp.sqrt(gravity * jnp.maximum(water_top, depth_floor)) * (
        bnd_surface - (bed_top + water_top)
    )


def blend(levels_stack, fine_index):
    lower = fine_index // SUB
    weight = (fine_index % SUB + 1) / SUB
    return (1.0 - weight) * levels_stack[lower] + weight * levels_stack[lower + 1]


def per_device(c_eta, c_flux, c_depth, f_bed, f_depth, f_wet, f_class, manning, nest_map):
    row_index = lax.axis_index("rows")
    col_index = lax.axis_index("cols")
    row_count = lax.axis_size("rows")
    col_count = lax.axis_size("cols")
    tile_rows, tile_cols = c_eta.shape
    fine_rows_dev, fine_cols_dev = f_bed.shape
    coarse_width = tile_cols * col_count
    coarse_row = nest_map // coarse_width
    coarse_col = nest_map % coarse_width
    local_row = coarse_row - row_index * tile_rows
    local_col = coarse_col - col_index * tile_cols
    owned = (local_row >= 0) & (local_row < tile_rows) & (local_col >= 0) & (local_col < tile_cols)
    flat_index = jnp.where(owned, local_row * tile_cols + local_col, 0)
    owned_weight = jnp.where(owned, 1.0, 0.0)

    def sample(surface, rows_flux):
        velocity = rows_flux / (c_depth + surface)
        return jnp.stack(
            [
                jnp.take(surface.reshape(-1), flat_index) * owned_weight,
                jnp.take(velocity.reshape(-1), flat_index) * owned_weight,
            ]
        )

    surface = c_eta
    rows_flux = c_flux[0]
    cols_flux = c_flux[1]
    sampled = [sample(surface, rows_flux)]
    for coarse_index in range(CSTEPS):
        stacked = jnp.stack([surface, c_depth + surface, rows_flux, cols_flux])
        padded = padded_2(stacked, (("rows", 1), ("cols", 2)), 1)
        surface, rows_flux, cols_flux = coarse_update(padded)
        sampled.append(sample(surface, rows_flux))
    levels_stack = jnp.stack(sampled)
    per_step = jnp.stack([blend(levels_stack, fine_index) for fine_index in range(FSTEPS)])
    summed = lax.psum(per_step, ("rows", "cols"))
    boundary = lax.dynamic_slice_in_dim(summed, col_index * fine_cols_dev, fine_cols_dev, 2)
    roughness = jnp.zeros_like(f_bed)
    for class_index in range(NCLASS):
        roughness = jnp.where(f_class == class_index, manning[class_index], roughness)
    water = f_wet.astype(f_bed.dtype) * f_depth
    fine_rows = jnp.zeros_like(water)
    fine_cols = jnp.zeros_like(water)
    fine_tick = coarse_tick / SUB
    row_start = row_index * fine_rows_dev
    col_start = col_index * fine_cols_dev
    total_rows = fine_rows_dev * row_count
    total_cols = fine_cols_dev * col_count
    col_faces = col_start + jnp.arange(fine_cols_dev + 1)
    col_keep = jnp.where((col_faces == 0) | (col_faces == total_cols), 0.0, 1.0)[None, :]
    static_pad = padded_2(jnp.stack([f_bed, roughness]), (("rows", 1), ("cols", 2)), 1)
    bed_pad = static_pad[0]
    rough_pad = static_pad[1]
    row_faces = row_start + jnp.arange(fine_rows_dev + 1)
    row_keep = jnp.where(row_faces == total_rows, 0.0, 1.0)[:, None]
    at_top = row_index == 0
    for fine_index in range(FSTEPS):
        state_pad = padded_2(
            jnp.stack([water, fine_rows, fine_cols]), (("rows", 1), ("cols", 2)), 1
        )
        water_pad = state_pad[0]
        new_rows, new_cols = fine_faces(
            water_pad, bed_pad, rough_pad, state_pad[1], state_pad[2], fine_tick
        )
        new_rows = new_rows * row_keep
        new_cols = new_cols * col_keep
        top_flux = open_boundary(
            water_pad[1, 1:-1], bed_pad[1, 1:-1], boundary[fine_index, 0], boundary[fine_index, 1]
        )
        first_face = jnp.where(at_top, top_flux, new_rows[0])
        new_rows = jnp.concatenate([first_face[None, :], new_rows[1:]], axis=0)
        water = water_pad[1:-1, 1:-1] - fine_tick / fine_spacing * (
            new_rows[1:] - new_rows[:-1] + (new_cols[:, 1:] - new_cols[:, :-1])
        )
        fine_rows = new_rows[1:]
        fine_cols = new_cols[:, 1:]
    return (surface, water, jnp.stack([fine_rows, fine_cols]))


def solution(mesh):
    in_specs = (
        P("rows", "cols"),
        P(None, "rows", "cols"),
        P("rows", "cols"),
        P("rows", "cols"),
        P("rows", "cols"),
        P("rows", "cols"),
        P("rows", "cols"),
        P(),
        P(),
    )
    out_specs = (P("rows", "cols"), P("rows", "cols"), P(None, "rows", "cols"))
    return jax.shard_map(
        per_device, mesh=mesh, in_specs=in_specs, out_specs=out_specs, check_vma=False
    )
```

profile of v0, /device:TPU:1, one launch (start us, length us, event | category | flops | bytes accessed | tf_op | source)
XLA Modules:
  0.0 376.3 jit_solution(18096316524865931316)
XLA Ops:
  7.2 1.1 fusion.22
  8.4 3.9 %collective-permute-start = (f32[4,1,256]{2,1,0:T(1,128)S(1)}, f32[4,1,256]{2,1,0:T(1,128)S(1)}, u32[]{:S(2)}, u32[]{:S(2)}) collective-permute-start(f32[4,1,256]{2,1,0:T(1,128)S(1)} %get-tuple-element.32), channel_id=1, source_target_pairs={{0,8},{8,16},{16,24},{1,9},{9,17},{17,25},{2,10},{10,18},{18,26},{... | collective-permute-start | bytes 12296 | tf_op jit(solution)/shard_map/ppermute | solution.py:23
  12.4 1.3 collective-permute-start.1
  14.4 7.0 %select_bitcast_fusion = f32[1,32,256]{2,1,0:T(8,128)S(1)} fusion(s32[32,256]{1,0:T(8,128)S(1)} %copy-done.9, f32[]{:T(128)} %bitcast.27, f32[]{:T(128)} %bitcast.26, f32[]{:T(128)} %bitcast.25, f32[]{:T(128)} %bitcast.24, f32[]{:T(128)} %bitcast.23, f32[]{:T(128)} %bitcast.22, f32[]{:T(128)} %bitcast.21, f32[]{:T(128)} %bitcast.20, f32[]{:T(128)} %bitcast.19, ...), kind=kLoop, calls=%fused_computation.156 | loop fusion | flops 180224 | bytes 65580 | tf_op jit(solution)/shard_map/stack | solution.py:147
  21.4 4.0 %collective-permute-start.12 = (f32[2,1,256]{2,1,0:T(1,128)S(1)}, f32[2,1,256]{2,1,0:T(1,128)S(1)}, u32[]{:S(2)}, u32[]{:S(2)}) collective-permute-start(f32[2,1,256]{2,1,0:T(1,128)S(1)} %get-tuple-element.82), channel_id=1, source_target_pairs={{0,8},{8,16},{16,24},{1,9},{9,17},{17,25},{2,10},{10,18},{18,26},{... | collective-permute-start | bytes 6152 | tf_op jit(solution)/shard_map/ppermute | solution.py:23
  25.4 1.3 collective-permute-start.13
  26.8 4.7 %collective-permute-start.8 = (f32[3,1,256]{2,1,0:T(1,128)S(1)}, f32[3,1,256]{2,1,0:T(1,128)S(1)}, u32[]{:S(2)}, u32[]{:S(2)}) collective-permute-start(f32[3,1,256]{2,1,0:T(1,128)S(1)} %get-tuple-element.108), channel_id=1, source_target_pairs={{0,8},{8,16},{16,24},{1,9},{9,17},{17,25},{2,10},{10,18},{18,26},{... | collective-permute-start | bytes 9224 | tf_op jit(solution)/shard_map/ppermute | solution.py:23
  32.3 11.8 %gather_fusion.1 = f32[2048]{0:T(1024)S(1)} fusion(f32[32768]{0:T(1024)S(1)} %bitcast.271, s32[2048]{0:T(1024)S(1)} %get-tuple-element.10), kind=kCustom, calls=%fused_computation.1.clone | custom fusion | bytes 24576 | tf_op jit(solution)/shard_map/jit(_take)/gather | solution.py:117
  44.1 11.8 %gather_fusion = f32[2048]{0:T(1024)S(1)} fusion(f32[32768]{0:T(1024)S(1)} %bitcast.272, s32[2048]{0:T(1024)S(1)} %get-tuple-element.10), kind=kCustom, calls=%fused_computation.clone | custom fusion | bytes 24576 | tf_op jit(solution)/shard_map/jit(_take)/gather | solution.py:116
  56.0 4.9 %collective-permute-start.14 = (f32[2,34,1]{2,1,0:T(8,128)S(1)}, f32[2,34,1]{2,1,0:T(8,128)S(1)}, u32[]{:S(2)}, u32[]{:S(2)}) collective-permute-start(f32[2,34,1]{2,1,0:T(8,128)S(1)} %get-tuple-element.80), channel_id=1, source_target_pairs={{0,1},{1,2},{2,3},{3,4},{4,5},{5,6},{6,7},{8,9},{9,10},{10,11},{11... | collective-permute-start | bytes 824 | tf_op jit(solution)/shard_map/ppermute | solution.py:23
  60.9 1.9 collective-permute-start.15
  62.9 1.3 collective-permute-start.9
  64.2 2.3 collective-permute-done.15
  66.6 1.8 collective-permute-done.9
  68.5 4.5 %collective-permute-start.10 = (f32[3,34,1]{2,1,0:T(8,128)S(1)}, f32[3,34,1]{2,1,0:T(8,128)S(1)}, u32[]{:S(2)}, u32[]{:S(2)}) collective-permute-start(f32[3,34,1]{2,1,0:T(8,128)S(1)} %get-tuple-element.68), channel_id=1, source_target_pairs={{0,1},{1,2},{2,3},{3,4},{4,5},{5,6},{6,7},{8,9},{9,10},{10,11},{11... | collective-permute-start | bytes 1232 | tf_op jit(solution)/shard_map/ppermute | solution.py:23
  73.0 1.9 collective-permute-start.11
  75.0 3.6 collective-permute-done.11
  78.9 1.9 collective-permute-start.2
  80.9 2.4 collective-permute-start.3
  83.3 1.0 collective-permute-done.2
  84.3 4.4 %collective-permute-done.3 = f32[4,130,1]{2,1,0:T(8,128)S(1)} collective-permute-done((f32[4,130,1]{2,1,0:T(8,128)S(1)}, f32[4,130,1]{2,1,0:T(8,128)S(1)}, u32[]{:S(2)}, u32[]{:S(2)}) %collective-permute-start.3) | collective-permute-done | bytes 2112 | tf_op jit(solution)/shard_map/ppermute | solution.py:26
  90.5 4.5 %collective-permute-start.4 = (f32[4,1,256]{2,1,0:T(1,128)S(1)}, f32[4,1,256]{2,1,0:T(1,128)S(1)}, u32[]{:S(2)}, u32[]{:S(2)}) collective-permute-start(f32[4,1,256]{2,1,0:T(1,128)S(1)} %get-tuple-element.30), channel_id=1, source_target_pairs={{0,8},{8,16},{16,24},{1,9},{9,17},{17,25},{2,10},{10,18},{18,26},{... | collective-permute-start | bytes 12296 | tf_op jit(solution)/shard_map/ppermute | solution.py:23
  95.1 1.3 collective-permute-start.5
  96.5 2.9 collective-permute-done.5
  99.6 3.2 collective-permute-start.6
  102.8 1.9 collective-permute-start.7
  105.0 11.8 %gather_fusion.2 = f32[2048]{0:T(1024)S(1)} fusion(f32[32768]{0:T(1024)S(1)} %bitcast.275, s32[2048]{0:T(1024)S(1)} %get-tuple-element.10), kind=kCustom, calls=%fused_computation.2.clone | custom fusion | bytes 24576 | tf_op jit(solution)/shard_map/jit(_take)/gather | solution.py:116
  116.8 11.8 %gather_fusion.3 = f32[2048]{0:T(1024)S(1)} fusion(f32[32768]{0:T(1024)S(1)} %bitcast.274, s32[2048]{0:T(1024)S(1)} %get-tuple-element.10), kind=kCustom, calls=%fused_computation.3.clone | custom fusion | bytes 24576 | tf_op jit(solution)/shard_map/jit(_take)/gather | solution.py:117
  130.4 11.8 %gather_fusion.4 = f32[2048]{0:T(1024)S(1)} fusion(f32[32768]{0:T(1024)S(1)} %bitcast.276, s32[2048]{0:T(1024)S(1)} %get-tuple-element.10), kind=kCustom, calls=%fused_computation.4.clone | custom fusion | bytes 24576 | tf_op jit(solution)/shard_map/jit(_take)/gather | solution.py:116
  142.2 11.8 %gather_fusion.5 = f32[2048]{0:T(1024)S(1)} fusion(f32[32768]{0:T(1024)S(1)} %bitcast.273, s32[2048]{0:T(1024)S(1)} %get-tuple-element.10), kind=kCustom, calls=%fused_computation.5.clone | custom fusion | bytes 24576 | tf_op jit(solution)/shard_map/jit(_take)/gather | solution.py:117
  155.0 120.0 %all-reduce.3.cloned.1.call-done = f32[6,2,2048]{2,1,0:T(2,128)} async-done(((f32[6,2,2048]{2,1,0:T(2,128)}), f32[6,2,2048]{2,1,0:T(2,128)}) %all-reduce.3.cloned.1.call-update) | async-done | bytes 98320 | tf_op jit(solution)/shard_map/psum | solution.py:132
  276.0 3.1 collective-permute-start.16
  279.1 1.3 collective-permute-start.17
  280.4 3.0 collective-permute-done.17
  283.5 7.1 %collective-permute-start.18 = (f32[3,34,1]{2,1,0:T(8,128)S(1)}, f32[3,34,1]{2,1,0:T(8,128)S(1)}, u32[]{:S(2)}, u32[]{:S(2)}) collective-permute-start(f32[3,34,1]{2,1,0:T(8,128)S(1)} %get-tuple-element.64), channel_id=1, source_target_pairs={{0,1},{1,2},{2,3},{3,4},{4,5},{5,6},{6,7},{8,9},{9,10},{10,11},{11... | collective-permute-start | bytes 1232 | tf_op jit(solution)/shard_map/ppermute | solution.py:23
  290.7 1.9 collective-permute-start.19
  292.6 3.6 collective-permute-done.19
  296.7 0.9 broadcast_select_fusion.4
  297.7 4.0 %collective-permute-start.20 = (f32[3,1,256]{2,1,0:T(1,128)S(1)}, f32[3,1,256]{2,1,0:T(1,128)S(1)}, u32[]{:S(2)}, u32[]{:S(2)}) collective-permute-start(f32[3,1,256]{2,1,0:T(1,128)S(1)} %get-tuple-element.76), channel_id=1, source_target_pairs={{0,8},{8,16},{16,24},{1,9},{9,17},{17,25},{2,10},{10,18},{18,26},{... | collective-permute-start | bytes 9224 | tf_op jit(solution)/shard_map/ppermute | solution.py:23
  301.7 1.3 collective-permute-start.21
  303.0 3.0 collective-permute-done.21
  306.1 3.3 collective-permute-start.22
  309.4 1.9 collective-permute-start.23
  311.4 3.6 collective-permute-done.23
  315.5 0.8 broadcast_select_fusion.3
  316.4 2.5 collective-permute-start.24
  319.0 1.3 collective-permute-start.25
  320.3 3.0 collective-permute-done.25
  323.4 3.3 collective-permute-start.26
  326.7 1.9 collective-permute-start.27
  328.6 3.6 collective-permute-done.27
  332.7 0.8 broadcast_select_fusion.2
  333.7 2.5 collective-permute-start.28
  336.2 1.3 collective-permute-start.29
  337.6 3.0 collective-permute-done.29
  340.7 3.3 collective-permute-start.30
  344.0 1.9 collective-permute-start.31
  345.9 3.6 collective-permute-done.31
  351.0 2.5 collective-permute-start.32
  353.5 1.3 collective-permute-start.33
  354.8 3.0 collective-permute-done.33
  357.9 3.3 collective-permute-start.34
  361.3 1.9 collective-permute-start.35
  363.2 3.6 collective-permute-done.35
  (150 shorter events, 14.6 us)
Async XLA Ops:
  7.2 1.2 copy-start
  7.2 1.2 copy-start.1
  7.2 267.9 %all-reduce.3.cloned.1.call-start = ((), (), s32[]{:S(2)}) async-start(), calls=%async_computation | async-start | bytes 196608 | tf_op jit(solution)/shard_map/psum | solution.py:132
  8.4 5.3 %copy-start.6 = (f32[11]{0:T(128)S(1)}, f32[11]{0:T(128)}, u32[]{:S(2)}) copy-start(f32[11]{0:T(128)} %param.18) | copy-start | bytes 136
  8.4 6.0 %copy-start.9 = (s32[32,256]{1,0:T(8,128)S(1)}, s32[32,256]{1,0:T(8,128)}, u32[]{:S(2)}) copy-start(s32[32,256]{1,0:T(8,128)} %param.17) | copy-start | bytes 98308
  8.4 70.3 %collective-permute-start = (f32[4,1,256]{2,1,0:T(1,128)S(1)}, f32[4,1,256]{2,1,0:T(1,128)S(1)}, u32[]{:S(2)}, u32[]{:S(2)}) collective-permute-start(f32[4,1,256]{2,1,0:T(1,128)S(1)} %get-tuple-element.32), channel_id=1, source_target_pairs={{0,8},{8,16},{16,24},{1,9},{9,17},{17,25},{2,10},{10,18},{18,26},{... | collective-permute-start | bytes 12296 | tf_op jit(solution)/shard_map/ppermute | solution.py:23
  12.4 66.4 %collective-permute-start.1 = (f32[4,1,256]{2,1,0:T(1,128)S(1)}, f32[4,1,256]{2,1,0:T(1,128)S(1)}, u32[]{:S(2)}, u32[]{:S(2)}) collective-permute-start(f32[4,1,256]{2,1,0:T(1,128)S(1)} %get-tuple-element.33), channel_id=1, source_target_pairs={{8,0},{16,8},{24,16},{9,1},{17,9},{25,17},{10,2},{18,10},{26,18},{... | collective-permute-start | bytes 12296 | tf_op jit(solution)/shard_map/ppermute | solution.py:26
  14.4 7.0 %copy-start.4 = (f32[32,256]{1,0:T(8,128)S(1)}, f32[32,256]{1,0:T(8,128)}, u32[]{:S(2)}) copy-start(f32[32,256]{1,0:T(8,128)} %param.14) | copy-start | bytes 98308
  21.4 5.3 %copy-start.7 = (f32[32,256]{1,0:T(8,128)S(1)}, f32[32,256]{1,0:T(8,128)}, u32[]{:S(2)}) copy-start(f32[32,256]{1,0:T(8,128)} %param.15) | copy-start | bytes 98308
  21.4 5.3 %copy-start.8 = (s32[32,256]{1,0:T(8,128)S(1)}, s32[32,256]{1,0:T(8,128)}, u32[]{:S(2)}) copy-start(s32[32,256]{1,0:T(8,128)} %param.16) | copy-start | bytes 98308
  21.4 34.5 %collective-permute-start.12 = (f32[2,1,256]{2,1,0:T(1,128)S(1)}, f32[2,1,256]{2,1,0:T(1,128)S(1)}, u32[]{:S(2)}, u32[]{:S(2)}) collective-permute-start(f32[2,1,256]{2,1,0:T(1,128)S(1)} %get-tuple-element.82), channel_id=1, source_target_pairs={{0,8},{8,16},{16,24},{1,9},{9,17},{17,25},{2,10},{10,18},{18,26},{... | collective-permute-start | bytes 6152 | tf_op jit(solution)/shard_map/ppermute | solution.py:23
  25.4 30.5 %collective-permute-start.13 = (f32[2,1,256]{2,1,0:T(1,128)S(1)}, f32[2,1,256]{2,1,0:T(1,128)S(1)}, u32[]{:S(2)}, u32[]{:S(2)}) collective-permute-start(f32[2,1,256]{2,1,0:T(1,128)S(1)} %get-tuple-element.83), channel_id=1, source_target_pairs={{8,0},{16,8},{24,16},{9,1},{17,9},{25,17},{10,2},{18,10},{26,18},{... | collective-permute-start | bytes 6152 | tf_op jit(solution)/shard_map/ppermute | solution.py:26
  26.8 39.8 %collective-permute-start.8 = (f32[3,1,256]{2,1,0:T(1,128)S(1)}, f32[3,1,256]{2,1,0:T(1,128)S(1)}, u32[]{:S(2)}, u32[]{:S(2)}) collective-permute-start(f32[3,1,256]{2,1,0:T(1,128)S(1)} %get-tuple-element.108), channel_id=1, source_target_pairs={{0,8},{8,16},{16,24},{1,9},{9,17},{17,25},{2,10},{10,18},{18,26},{... | collective-permute-start | bytes 9224 | tf_op jit(solution)/shard_map/ppermute | solution.py:23
  31.4 0.7 copy-start.10
  56.0 6.8 %collective-permute-start.14 = (f32[2,34,1]{2,1,0:T(8,128)S(1)}, f32[2,34,1]{2,1,0:T(8,128)S(1)}, u32[]{:S(2)}, u32[]{:S(2)}) collective-permute-start(f32[2,34,1]{2,1,0:T(8,128)S(1)} %get-tuple-element.80), channel_id=1, source_target_pairs={{0,1},{1,2},{2,3},{3,4},{4,5},{5,6},{6,7},{8,9},{9,10},{10,11},{11... | collective-permute-start | bytes 824 | tf_op jit(solution)/shard_map/ppermute | solution.py:23
  60.9 5.5 %collective-permute-start.15 = (f32[2,34,1]{2,1,0:T(8,128)S(1)}, f32[2,34,1]{2,1,0:T(8,128)S(1)}, u32[]{:S(2)}, u32[]{:S(2)}) collective-permute-start(f32[2,34,1]{2,1,0:T(8,128)S(1)} %get-tuple-element.81), channel_id=1, source_target_pairs={{1,0},{2,1},{3,2},{4,3},{5,4},{6,5},{7,6},{9,8},{10,9},{11,10},{12... | collective-permute-start | bytes 824 | tf_op jit(solution)/shard_map/ppermute | solution.py:26
  62.9 5.5 %collective-permute-start.9 = (f32[3,1,256]{2,1,0:T(1,128)S(1)}, f32[3,1,256]{2,1,0:T(1,128)S(1)}, u32[]{:S(2)}, u32[]{:S(2)}) collective-permute-start(f32[3,1,256]{2,1,0:T(1,128)S(1)} %get-tuple-element.109), channel_id=1, source_target_pairs={{8,0},{16,8},{24,16},{9,1},{17,9},{25,17},{10,2},{18,10},{26,18},{... | collective-permute-start | bytes 9224 | tf_op jit(solution)/shard_map/ppermute | solution.py:26
  68.5 6.5 %collective-permute-start.10 = (f32[3,34,1]{2,1,0:T(8,128)S(1)}, f32[3,34,1]{2,1,0:T(8,128)S(1)}, u32[]{:S(2)}, u32[]{:S(2)}) collective-permute-start(f32[3,34,1]{2,1,0:T(8,128)S(1)} %get-tuple-element.68), channel_id=1, source_target_pairs={{0,1},{1,2},{2,3},{3,4},{4,5},{5,6},{6,7},{8,9},{9,10},{10,11},{11... | collective-permute-start | bytes 1232 | tf_op jit(solution)/shard_map/ppermute | solution.py:23
  73.0 5.5 %collective-permute-start.11 = (f32[3,34,1]{2,1,0:T(8,128)S(1)}, f32[3,34,1]{2,1,0:T(8,128)S(1)}, u32[]{:S(2)}, u32[]{:S(2)}) collective-permute-start(f32[3,34,1]{2,1,0:T(8,128)S(1)} %get-tuple-element.69), channel_id=1, source_target_pairs={{1,0},{2,1},{3,2},{4,3},{5,4},{6,5},{7,6},{9,8},{10,9},{11,10},{12... | collective-permute-start | bytes 1232 | tf_op jit(solution)/shard_map/ppermute | solution.py:26
  78.9 5.4 %collective-permute-start.2 = (f32[4,130,1]{2,1,0:T(8,128)S(1)}, f32[4,130,1]{2,1,0:T(8,128)S(1)}, u32[]{:S(2)}, u32[]{:S(2)}) collective-permute-start(f32[4,130,1]{2,1,0:T(8,128)S(1)} %get-tuple-element.28), channel_id=1, source_target_pairs={{0,1},{1,2},{2,3},{3,4},{4,5},{5,6},{6,7},{8,9},{9,10},{10,11},{11... | collective-permute-start | bytes 6248 | tf_op jit(solution)/shard_map/ppermute | solution.py:23
  80.9 7.9 %collective-permute-start.3 = (f32[4,130,1]{2,1,0:T(8,128)S(1)}, f32[4,130,1]{2,1,0:T(8,128)S(1)}, u32[]{:S(2)}, u32[]{:S(2)}) collective-permute-start(f32[4,130,1]{2,1,0:T(8,128)S(1)} %get-tuple-element.29), channel_id=1, source_target_pairs={{1,0},{2,1},{3,2},{4,3},{5,4},{6,5},{7,6},{9,8},{10,9},{11,10},{12... | collective-permute-start | bytes 6248 | tf_op jit(solution)/shard_map/ppermute | solution.py:26
  89.4 0.9 copy-start.2
  90.5 6.0 %collective-permute-start.4 = (f32[4,1,256]{2,1,0:T(1,128)S(1)}, f32[4,1,256]{2,1,0:T(1,128)S(1)}, u32[]{:S(2)}, u32[]{:S(2)}) collective-permute-start(f32[4,1,256]{2,1,0:T(1,128)S(1)} %get-tuple-element.30), channel_id=1, source_target_pairs={{0,8},{8,16},{16,24},{1,9},{9,17},{17,25},{2,10},{10,18},{18,26},{... | collective-permute-start | bytes 12296 | tf_op jit(solution)/shard_map/ppermute | solution.py:23
  95.1 4.4 %collective-permute-start.5 = (f32[4,1,256]{2,1,0:T(1,128)S(1)}, f32[4,1,256]{2,1,0:T(1,128)S(1)}, u32[]{:S(2)}, u32[]{:S(2)}) collective-permute-start(f32[4,1,256]{2,1,0:T(1,128)S(1)} %get-tuple-element.31), channel_id=1, source_target_pairs={{8,0},{16,8},{24,16},{9,1},{17,9},{25,17},{10,2},{18,10},{26,18},{... | collective-permute-start | bytes 12296 | tf_op jit(solution)/shard_map/ppermute | solution.py:26
  99.6 29.0 %collective-permute-start.6 = (f32[4,130,1]{2,1,0:T(8,128)S(1)}, f32[4,130,1]{2,1,0:T(8,128)S(1)}, u32[]{:S(2)}, u32[]{:S(2)}) collective-permute-start(f32[4,130,1]{2,1,0:T(8,128)S(1)} %get-tuple-element.26), channel_id=1, source_target_pairs={{0,1},{1,2},{2,3},{3,4},{4,5},{5,6},{6,7},{8,9},{9,10},{10,11},{11... | collective-permute-start | bytes 6248 | tf_op jit(solution)/shard_map/ppermute | solution.py:23
  102.8 25.8 %collective-permute-start.7 = (f32[4,130,1]{2,1,0:T(8,128)S(1)}, f32[4,130,1]{2,1,0:T(8,128)S(1)}, u32[]{:S(2)}, u32[]{:S(2)}) collective-permute-start(f32[4,130,1]{2,1,0:T(8,128)S(1)} %get-tuple-element.27), channel_id=1, source_target_pairs={{1,0},{2,1},{3,2},{4,3},{5,4},{6,5},{7,6},{9,8},{10,9},{11,10},{12... | collective-permute-start | bytes 6248 | tf_op jit(solution)/shard_map/ppermute | solution.py:26
  129.7 0.7 copy-start.3
  154.4 0.6 copy-start.5
  276.0 4.4 %collective-permute-start.16 = (f32[3,1,256]{2,1,0:T(1,128)S(1)}, f32[3,1,256]{2,1,0:T(1,128)S(1)}, u32[]{:S(2)}, u32[]{:S(2)}) collective-permute-start(f32[3,1,256]{2,1,0:T(1,128)S(1)} %get-tuple-element.78), channel_id=1, source_target_pairs={{0,8},{8,16},{16,24},{1,9},{9,17},{17,25},{2,10},{10,18},{18,26},{... | collective-permute-start | bytes 9224 | tf_op jit(solution)/shard_map/ppermute | solution.py:23
  279.1 4.3 %collective-permute-start.17 = (f32[3,1,256]{2,1,0:T(1,128)S(1)}, f32[3,1,256]{2,1,0:T(1,128)S(1)}, u32[]{:S(2)}, u32[]{:S(2)}) collective-permute-start(f32[3,1,256]{2,1,0:T(1,128)S(1)} %get-tuple-element.79), channel_id=1, source_target_pairs={{8,0},{16,8},{24,16},{9,1},{17,9},{25,17},{10,2},{18,10},{26,18},{... | collective-permute-start | bytes 9224 | tf_op jit(solution)/shard_map/ppermute | solution.py:26
  283.5 9.1 %collective-permute-start.18 = (f32[3,34,1]{2,1,0:T(8,128)S(1)}, f32[3,34,1]{2,1,0:T(8,128)S(1)}, u32[]{:S(2)}, u32[]{:S(2)}) collective-permute-start(f32[3,34,1]{2,1,0:T(8,128)S(1)} %get-tuple-element.64), channel_id=1, source_target_pairs={{0,1},{1,2},{2,3},{3,4},{4,5},{5,6},{6,7},{8,9},{9,10},{10,11},{11... | collective-permute-start | bytes 1232 | tf_op jit(solution)/shard_map/ppermute | solution.py:23
  290.7 5.5 %collective-permute-start.19 = (f32[3,34,1]{2,1,0:T(8,128)S(1)}, f32[3,34,1]{2,1,0:T(8,128)S(1)}, u32[]{:S(2)}, u32[]{:S(2)}) collective-permute-start(f32[3,34,1]{2,1,0:T(8,128)S(1)} %get-tuple-element.65), channel_id=1, source_target_pairs={{1,0},{2,1},{3,2},{4,3},{5,4},{6,5},{7,6},{9,8},{10,9},{11,10},{12... | collective-permute-start | bytes 1232 | tf_op jit(solution)/shard_map/ppermute | solution.py:26
  297.7 5.3 %collective-permute-start.20 = (f32[3,1,256]{2,1,0:T(1,128)S(1)}, f32[3,1,256]{2,1,0:T(1,128)S(1)}, u32[]{:S(2)}, u32[]{:S(2)}) collective-permute-start(f32[3,1,256]{2,1,0:T(1,128)S(1)} %get-tuple-element.76), channel_id=1, source_target_pairs={{0,8},{8,16},{16,24},{1,9},{9,17},{17,25},{2,10},{10,18},{18,26},{... | collective-permute-start | bytes 9224 | tf_op jit(solution)/shard_map/ppermute | solution.py:23
  301.7 4.3 %collective-permute-start.21 = (f32[3,1,256]{2,1,0:T(1,128)S(1)}, f32[3,1,256]{2,1,0:T(1,128)S(1)}, u32[]{:S(2)}, u32[]{:S(2)}) collective-permute-start(f32[3,1,256]{2,1,0:T(1,128)S(1)} %get-tuple-element.77), channel_id=1, source_target_pairs={{8,0},{16,8},{24,16},{9,1},{17,9},{25,17},{10,2},{18,10},{26,18},{... | collective-permute-start | bytes 9224 | tf_op jit(solution)/shard_map/ppermute | solution.py:26
  306.1 5.2 %collective-permute-start.22 = (f32[3,34,1]{2,1,0:T(8,128)S(1)}, f32[3,34,1]{2,1,0:T(8,128)S(1)}, u32[]{:S(2)}, u32[]{:S(2)}) collective-permute-start(f32[3,34,1]{2,1,0:T(8,128)S(1)} %get-tuple-element.62), channel_id=1, source_target_pairs={{0,1},{1,2},{2,3},{3,4},{4,5},{5,6},{6,7},{8,9},{9,10},{10,11},{11... | collective-permute-start | bytes 1232 | tf_op jit(solution)/shard_map/ppermute | solution.py:23
  309.4 5.5 %collective-permute-start.23 = (f32[3,34,1]{2,1,0:T(8,128)S(1)}, f32[3,34,1]{2,1,0:T(8,128)S(1)}, u32[]{:S(2)}, u32[]{:S(2)}) collective-permute-start(f32[3,34,1]{2,1,0:T(8,128)S(1)} %get-tuple-element.63), channel_id=1, source_target_pairs={{1,0},{2,1},{3,2},{4,3},{5,4},{6,5},{7,6},{9,8},{10,9},{11,10},{12... | collective-permute-start | bytes 1232 | tf_op jit(solution)/shard_map/ppermute | solution.py:26
  316.4 3.9 %collective-permute-start.24 = (f32[3,1,256]{2,1,0:T(1,128)S(1)}, f32[3,1,256]{2,1,0:T(1,128)S(1)}, u32[]{:S(2)}, u32[]{:S(2)}) collective-permute-start(f32[3,1,256]{2,1,0:T(1,128)S(1)} %get-tuple-element.74), channel_id=1, source_target_pairs={{0,8},{8,16},{16,24},{1,9},{9,17},{17,25},{2,10},{10,18},{18,26},{... | collective-permute-start | bytes 9224 | tf_op jit(solution)/shard_map/ppermute | solution.py:23
  319.0 4.3 %collective-permute-start.25 = (f32[3,1,256]{2,1,0:T(1,128)S(1)}, f32[3,1,256]{2,1,0:T(1,128)S(1)}, u32[]{:S(2)}, u32[]{:S(2)}) collective-permute-start(f32[3,1,256]{2,1,0:T(1,128)S(1)} %get-tuple-element.75), channel_id=1, source_target_pairs={{8,0},{16,8},{24,16},{9,1},{17,9},{25,17},{10,2},{18,10},{26,18},{... | collective-permute-start | bytes 9224 | tf_op jit(solution)/shard_map/ppermute | solution.py:26
  323.4 5.2 %collective-permute-start.26 = (f32[3,34,1]{2,1,0:T(8,128)S(1)}, f32[3,34,1]{2,1,0:T(8,128)S(1)}, u32[]{:S(2)}, u32[]{:S(2)}) collective-permute-start(f32[3,34,1]{2,1,0:T(8,128)S(1)} %get-tuple-element.60), channel_id=1, source_target_pairs={{0,1},{1,2},{2,3},{3,4},{4,5},{5,6},{6,7},{8,9},{9,10},{10,11},{11... | collective-permute-start | bytes 1232 | tf_op jit(solution)/shard_map/ppermute | solution.py:23
  326.7 5.5 %collective-permute-start.27 = (f32[3,34,1]{2,1,0:T(8,128)S(1)}, f32[3,34,1]{2,1,0:T(8,128)S(1)}, u32[]{:S(2)}, u32[]{:S(2)}) collective-permute-start(f32[3,34,1]{2,1,0:T(8,128)S(1)} %get-tuple-element.61), channel_id=1, source_target_pairs={{1,0},{2,1},{3,2},{4,3},{5,4},{6,5},{7,6},{9,8},{10,9},{11,10},{12... | collective-permute-start | bytes 1232 | tf_op jit(solution)/shard_map/ppermute | solution.py:26
  333.7 3.9 %collective-permute-start.28 = (f32[3,1,256]{2,1,0:T(1,128)S(1)}, f32[3,1,256]{2,1,0:T(1,128)S(1)}, u32[]{:S(2)}, u32[]{:S(2)}) collective-permute-start(f32[3,1,256]{2,1,0:T(1,128)S(1)} %get-tuple-element.72), channel_id=1, source_target_pairs={{0,8},{8,16},{16,24},{1,9},{9,17},{17,25},{2,10},{10,18},{18,26},{... | collective-permute-start | bytes 9224 | tf_op jit(solution)/shard_map/ppermute | solution.py:23
  336.2 4.3 %collective-permute-start.29 = (f32[3,1,256]{2,1,0:T(1,128)S(1)}, f32[3,1,256]{2,1,0:T(1,128)S(1)}, u32[]{:S(2)}, u32[]{:S(2)}) collective-permute-start(f32[3,1,256]{2,1,0:T(1,128)S(1)} %get-tuple-element.73), channel_id=1, source_target_pairs={{8,0},{16,8},{24,16},{9,1},{17,9},{25,17},{10,2},{18,10},{26,18},{... | collective-permute-start | bytes 9224 | tf_op jit(solution)/shard_map/ppermute | solution.py:26
  340.7 5.2 %collective-permute-start.30 = (f32[3,34,1]{2,1,0:T(8,128)S(1)}, f32[3,34,1]{2,1,0:T(8,128)S(1)}, u32[]{:S(2)}, u32[]{:S(2)}) collective-permute-start(f32[3,34,1]{2,1,0:T(8,128)S(1)} %get-tuple-element.58), channel_id=1, source_target_pairs={{0,1},{1,2},{2,3},{3,4},{4,5},{5,6},{6,7},{8,9},{9,10},{10,11},{11... | collective-permute-start | bytes 1232 | tf_op jit(solution)/shard_map/ppermute | solution.py:23
  344.0 5.5 %collective-permute-start.31 = (f32[3,34,1]{2,1,0:T(8,128)S(1)}, f32[3,34,1]{2,1,0:T(8,128)S(1)}, u32[]{:S(2)}, u32[]{:S(2)}) collective-permute-start(f32[3,34,1]{2,1,0:T(8,128)S(1)} %get-tuple-element.59), channel_id=1, source_target_pairs={{1,0},{2,1},{3,2},{4,3},{5,4},{6,5},{7,6},{9,8},{10,9},{11,10},{12... | collective-permute-start | bytes 1232 | tf_op jit(solution)/shard_map/ppermute | solution.py:26
  351.0 3.9 %collective-permute-start.32 = (f32[3,1,256]{2,1,0:T(1,128)S(1)}, f32[3,1,256]{2,1,0:T(1,128)S(1)}, u32[]{:S(2)}, u32[]{:S(2)}) collective-permute-start(f32[3,1,256]{2,1,0:T(1,128)S(1)} %get-tuple-element.70), channel_id=1, source_target_pairs={{0,8},{8,16},{16,24},{1,9},{9,17},{17,25},{2,10},{10,18},{18,26},{... | collective-permute-start | bytes 9224 | tf_op jit(solution)/shard_map/ppermute | solution.py:23
  353.5 4.3 %collective-permute-start.33 = (f32[3,1,256]{2,1,0:T(1,128)S(1)}, f32[3,1,256]{2,1,0:T(1,128)S(1)}, u32[]{:S(2)}, u32[]{:S(2)}) collective-permute-start(f32[3,1,256]{2,1,0:T(1,128)S(1)} %get-tuple-element.71), channel_id=1, source_target_pairs={{8,0},{16,8},{24,16},{9,1},{17,9},{25,17},{10,2},{18,10},{26,18},{... | collective-permute-start | bytes 9224 | tf_op jit(solution)/shard_map/ppermute | solution.py:26
  357.9 5.3 %collective-permute-start.34 = (f32[3,34,1]{2,1,0:T(8,128)S(1)}, f32[3,34,1]{2,1,0:T(8,128)S(1)}, u32[]{:S(2)}, u32[]{:S(2)}) collective-permute-start(f32[3,34,1]{2,1,0:T(8,128)S(1)} %get-tuple-element.56), channel_id=1, source_target_pairs={{0,1},{1,2},{2,3},{3,4},{4,5},{5,6},{6,7},{8,9},{9,10},{10,11},{11... | collective-permute-start | bytes 1232 | tf_op jit(solution)/shard_map/ppermute | solution.py:23
  361.3 5.5 %collective-permute-start.35 = (f32[3,34,1]{2,1,0:T(8,128)S(1)}, f32[3,34,1]{2,1,0:T(8,128)S(1)}, u32[]{:S(2)}, u32[]{:S(2)}) collective-permute-start(f32[3,34,1]{2,1,0:T(8,128)S(1)} %get-tuple-element.57), channel_id=1, source_target_pairs={{1,0},{2,1},{3,2},{4,3},{5,4},{6,5},{7,6},{9,8},{10,9},{11,10},{12... | collective-permute-start | bytes 1232 | tf_op jit(solution)/shard_map/ppermute | solution.py:26
Sparse Core Ops, SparseCore 0:
  155.1 119.8 all-reduce.2
where the time goes:
time: 378 us; the launch traced here: 376 us
  waiting for transfers between devices  169 us (45%)
  starting transfers between devices  96.1 us (25%)
  local copies, waits for them, and re-layouts  75.5 us (20%)
  other arithmetic  20.3 us (5%)
  between operations  15.2 us (4%)
    psum x1, waiting for transfers between devices, per_device(): summed = lax.psum(per_step, ('rows', 'cols'))  120 us
    ppermute x18, starting transfers between devices, padded_2(): lax.ppermute(lax.slice_in_dim(block, block.shape[dim] - width, None, axis...  66.7 us
    ppermute x18, waiting for transfers between devices, padded_2(): lax.ppermute(lax.slice_in_dim(block, 0, width, axis=dim), axis, backward)  48.1 us
    gather x3, local copies, waits for them, and re-layouts, sample(): jnp.take(velocity.reshape(-1), flat_index) * owned_weight  35.3 us
    gather x3, local copies, waits for them, and re-layouts, sample(): jnp.take(surface.reshape(-1), flat_index) * owned_weight  35.3 us
    ppermute x18, starting transfers between devices, padded_2(): lax.ppermute(lax.slice_in_dim(block, 0, width, axis=dim), axis, backward)  29.4 us
  transfers between devices with their start and end apart: 37, of which 17 were waited for; matrix products, arithmetic and copies ran while one was open for 15% of the time, Pallas kernels for 0%

commit v1 on v0

--- a/solution.py
+++ b/solution.py
@@ -129,7 +129,7 @@
         sampled.append(sample(surface, rows_flux))
     levels_stack = jnp.stack(sampled)
     per_step = jnp.stack([blend(levels_stack, fine_index) for fine_index in range(FSTEPS)])
-    summed = lax.psum(per_step, ("rows", "cols"))
+    summed = jnp.sum(lax.all_gather(per_step, ("rows", "cols")), axis=0)
     boundary = lax.dynamic_slice_in_dim(summed, col_index * fine_cols_dev, fine_cols_dev, 2)
     roughness = jnp.zeros_like(f_bed)
     for class_index in range(NCLASS):

time: 378 us -> 278 us (0.74)
  waiting for transfers between devices: 169 us -> 75.9 us
  starting transfers between devices: 96.1 us -> 90.9 us
    psum x1 -> x0, waiting for transfers between devices: 120 us -> none  [per_device(): summed = lax.psum(per_step, ('rows', 'cols'))]
    all_gather x0 -> x1, waiting for transfers between devices: none -> 23.2 us  [per_device(): summed = jnp.sum(lax.all_gather(per_step, ('rows', 'cols')), axis=0)]
    ppermute x18, starting transfers between devices: 66.7 us -> 61.4 us  [padded_2(): lax.ppermute(lax.slice_in_dim(block, block.shape[dim] - width, None, axis...]
    select_n x6, other arithmetic: 5.04 us -> 0.52 us  [per_device(): first_face = jnp.where(at_top, top_flux, new_rows[0])]
  transfers between devices with their start and end apart: 37 -> 37, of which waited for: 17 -> 17; matrix products, arithmetic and copies ran while one was open for 15% -> 20% of each run, Pallas kernels for 0% -> 0%
where the time goes in v1:
time: 278 us; the launch traced here: 277 us
  starting transfers between devices  90.9 us (33%)
  waiting for transfers between devices  75.9 us (27%)
  local copies, waits for them, and re-layouts  73.6 us (26%)
  other arithmetic  20.9 us (8%)
  between operations  15.3 us (6%)
    ppermute x18, starting transfers between devices, padded_2(): lax.ppermute(lax.slice_in_dim(block, block.shape[dim] - width, None, axis...  61.4 us
    ppermute x18, waiting for transfers between devices, padded_2(): lax.ppermute(lax.slice_in_dim(block, 0, width, axis=dim), axis, backward)  51 us
    gather x3, local copies, waits for them, and re-layouts, sample(): jnp.take(surface.reshape(-1), flat_index) * owned_weight  35.3 us
    gather x3, local copies, waits for them, and re-layouts, sample(): jnp.take(velocity.reshape(-1), flat_index) * owned_weight  35.3 us
    ppermute x18, starting transfers between devices, padded_2(): lax.ppermute(lax.slice_in_dim(block, 0, width, axis=dim), axis, backward)  29.4 us
    all_gather x1, waiting for transfers between devices, per_device(): summed = jnp.sum(lax.all_gather(per_step, ('rows', 'cols')), axis=0)  23.2 us
    another operation x1, other arithmetic, per_device(): jnp.stack([f_bed, roughness])  7.03 us
  transfers between devices with their start and end apart: 37, of which 17 were waited for; matrix products, arithmetic and copies ran while one was open for 20% of the time, Pallas kernels for 0%

profile of v1, /device:TPU:1, one launch (start us, length us, event | category | flops | bytes accessed | tf_op | source)
XLA Modules:
  0.0 276.5 jit_solution(15574919704762534328)
XLA Ops:
  7.2 1.1 fusion.22
  8.4 0.8 pad_maximum_fusion.34
  9.1 3.9 %collective-permute-start = (f32[4,1,256]{2,1,0:T(1,128)S(1)}, f32[4,1,256]{2,1,0:T(1,128)S(1)}, u32[]{:S(2)}, u32[]{:S(2)}) collective-permute-start(f32[4,1,256]{2,1,0:T(1,128)S(1)} %get-tuple-element.32), channel_id=1, source_target_pairs={{0,8},{8,16},{16,24},{1,9},{9,17},{17,25},{2,10},{10,18},{18,26},{... | collective-permute-start | bytes 12296 | tf_op jit(solution)/shard_map/ppermute | solution.py:23
  13.1 1.3 collective-permute-start.1
  14.4 3.0 %collective-permute-done.1 = f32[4,1,256]{2,1,0:T(1,128)S(1)} collective-permute-done((f32[4,1,256]{2,1,0:T(1,128)S(1)}, f32[4,1,256]{2,1,0:T(1,128)S(1)}, u32[]{:S(2)}, u32[]{:S(2)}) %collective-permute-start.1) | collective-permute-done | bytes 4128 | tf_op jit(solution)/shard_map/ppermute | solution.py:26
  17.4 1.0 pad_maximum_fusion.2
  18.6 5.2 %collective-permute-start.2 = (f32[4,130,1]{2,1,0:T(8,128)S(1)}, f32[4,130,1]{2,1,0:T(8,128)S(1)}, u32[]{:S(2)}, u32[]{:S(2)}) collective-permute-start(f32[4,130,1]{2,1,0:T(8,128)S(1)} %get-tuple-element.28), channel_id=1, source_target_pairs={{0,1},{1,2},{2,3},{3,4},{4,5},{5,6},{6,7},{8,9},{9,10},{10,11},{11... | collective-permute-start | bytes 6248 | tf_op jit(solution)/shard_map/ppermute | solution.py:23
  23.8 1.9 collective-permute-start.3
  25.7 1.5 collective-permute-done.2
  27.3 4.4 %collective-permute-done.3 = f32[4,130,1]{2,1,0:T(8,128)S(1)} collective-permute-done((f32[4,130,1]{2,1,0:T(8,128)S(1)}, f32[4,130,1]{2,1,0:T(8,128)S(1)}, u32[]{:S(2)}, u32[]{:S(2)}) %collective-permute-start.3) | collective-permute-done | bytes 2112 | tf_op jit(solution)/shard_map/ppermute | solution.py:26
  32.8 4.0 %collective-permute-start.4 = (f32[4,1,256]{2,1,0:T(1,128)S(1)}, f32[4,1,256]{2,1,0:T(1,128)S(1)}, u32[]{:S(2)}, u32[]{:S(2)}) collective-permute-start(f32[4,1,256]{2,1,0:T(1,128)S(1)} %get-tuple-element.30), channel_id=1, source_target_pairs={{0,8},{8,16},{16,24},{1,9},{9,17},{17,25},{2,10},{10,18},{18,26},{... | collective-permute-start | bytes 12296 | tf_op jit(solution)/shard_map/ppermute | solution.py:23
  36.8 1.3 collective-permute-start.5
  38.2 3.0 %collective-permute-done.5 = f32[4,1,256]{2,1,0:T(1,128)S(1)} collective-permute-done((f32[4,1,256]{2,1,0:T(1,128)S(1)}, f32[4,1,256]{2,1,0:T(1,128)S(1)}, u32[]{:S(2)}, u32[]{:S(2)}) %collective-permute-start.5) | collective-permute-done | bytes 4128 | tf_op jit(solution)/shard_map/ppermute | solution.py:26
  41.4 3.2 %collective-permute-start.6 = (f32[4,130,1]{2,1,0:T(8,128)S(1)}, f32[4,130,1]{2,1,0:T(8,128)S(1)}, u32[]{:S(2)}, u32[]{:S(2)}) collective-permute-start(f32[4,130,1]{2,1,0:T(8,128)S(1)} %get-tuple-element.26), channel_id=1, source_target_pairs={{0,1},{1,2},{2,3},{3,4},{4,5},{5,6},{6,7},{8,9},{9,10},{10,11},{11... | collective-permute-start | bytes 6248 | tf_op jit(solution)/shard_map/ppermute | solution.py:23
  44.6 1.9 collective-permute-start.7
  46.7 11.8 %gather_fusion.1 = f32[2048]{0:T(1024)S(1)} fusion(f32[32768]{0:T(1024)S(1)} %bitcast.272, s32[2048]{0:T(1024)S(1)} %get-tuple-element.10), kind=kCustom, calls=%fused_computation.1.clone | custom fusion | bytes 24576 | tf_op jit(solution)/shard_map/jit(_take)/gather | solution.py:117
  58.5 11.8 %gather_fusion = f32[2048]{0:T(1024)S(1)} fusion(f32[32768]{0:T(1024)S(1)} %bitcast.273, s32[2048]{0:T(1024)S(1)} %get-tuple-element.10), kind=kCustom, calls=%fused_computation.clone | custom fusion | bytes 24576 | tf_op jit(solution)/shard_map/jit(_take)/gather | solution.py:116
  70.4 11.8 %gather_fusion.2 = f32[2048]{0:T(1024)S(1)} fusion(f32[32768]{0:T(1024)S(1)} %bitcast.276, s32[2048]{0:T(1024)S(1)} %get-tuple-element.10), kind=kCustom, calls=%fused_computation.2.clone | custom fusion | bytes 24576 | tf_op jit(solution)/shard_map/jit(_take)/gather | solution.py:116
  82.2 11.8 %gather_fusion.3 = f32[2048]{0:T(1024)S(1)} fusion(f32[32768]{0:T(1024)S(1)} %bitcast.275, s32[2048]{0:T(1024)S(1)} %get-tuple-element.10), kind=kCustom, calls=%fused_computation.3.clone | custom fusion | bytes 24576 | tf_op jit(solution)/shard_map/jit(_take)/gather | solution.py:117
  95.2 11.8 %gather_fusion.4 = f32[2048]{0:T(1024)S(1)} fusion(f32[32768]{0:T(1024)S(1)} %bitcast.277, s32[2048]{0:T(1024)S(1)} %get-tuple-element.10), kind=kCustom, calls=%fused_computation.4.clone | custom fusion | bytes 24576 | tf_op jit(solution)/shard_map/jit(_take)/gather | solution.py:116
  107.1 11.8 %gather_fusion.5 = f32[2048]{0:T(1024)S(1)} fusion(f32[32768]{0:T(1024)S(1)} %bitcast.274, s32[2048]{0:T(1024)S(1)} %get-tuple-element.10), kind=kCustom, calls=%fused_computation.5.clone | custom fusion | bytes 24576 | tf_op jit(solution)/shard_map/jit(_take)/gather | solution.py:117
  120.6 7.0 %select_bitcast_fusion = f32[1,32,256]{2,1,0:T(8,128)S(1)} fusion(s32[32,256]{1,0:T(8,128)S(1)} %copy-done.9, f32[]{:T(128)} %bitcast.27, f32[]{:T(128)} %bitcast.26, f32[]{:T(128)} %bitcast.25, f32[]{:T(128)} %bitcast.24, f32[]{:T(128)} %bitcast.23, f32[]{:T(128)} %bitcast.22, f32[]{:T(128)} %bitcast.21, f32[]{:T(128)} %bitcast.20, f32[]{:T(128)} %bitcast.19, ...), kind=kLoop, calls=%fused_computation.156 | loop fusion | flops 180224 | bytes 65580 | tf_op jit(solution)/shard_map/stack | solution.py:147
  127.7 3.1 %collective-permute-start.12 = (f32[2,1,256]{2,1,0:T(1,128)S(1)}, f32[2,1,256]{2,1,0:T(1,128)S(1)}, u32[]{:S(2)}, u32[]{:S(2)}) collective-permute-start(f32[2,1,256]{2,1,0:T(1,128)S(1)} %get-tuple-element.82), channel_id=1, source_target_pairs={{0,8},{8,16},{16,24},{1,9},{9,17},{17,25},{2,10},{10,18},{18,26},{... | collective-permute-start | bytes 6152 | tf_op jit(solution)/shard_map/ppermute | solution.py:23
  130.8 1.3 collective-permute-start.13
  132.2 4.0 %collective-permute-start.8 = (f32[3,1,256]{2,1,0:T(1,128)S(1)}, f32[3,1,256]{2,1,0:T(1,128)S(1)}, u32[]{:S(2)}, u32[]{:S(2)}) collective-permute-start(f32[3,1,256]{2,1,0:T(1,128)S(1)} %get-tuple-element.108), channel_id=1, source_target_pairs={{0,8},{8,16},{16,24},{1,9},{9,17},{17,25},{2,10},{10,18},{18,26},{... | collective-permute-start | bytes 9224 | tf_op jit(solution)/shard_map/ppermute | solution.py:23
  136.1 1.3 collective-permute-start.9
  137.6 4.5 %collective-permute-start.14 = (f32[2,34,1]{2,1,0:T(8,128)S(1)}, f32[2,34,1]{2,1,0:T(8,128)S(1)}, u32[]{:S(2)}, u32[]{:S(2)}) collective-permute-start(f32[2,34,1]{2,1,0:T(8,128)S(1)} %get-tuple-element.80), channel_id=1, source_target_pairs={{0,1},{1,2},{2,3},{3,4},{4,5},{5,6},{6,7},{8,9},{9,10},{10,11},{11... | collective-permute-start | bytes 824 | tf_op jit(solution)/shard_map/ppermute | solution.py:23
  142.1 1.9 collective-permute-start.15
  144.0 3.4 %collective-permute-done.15 = f32[2,34,1]{2,1,0:T(8,128)S(1)} collective-permute-done((f32[2,34,1]{2,1,0:T(8,128)S(1)}, f32[2,34,1]{2,1,0:T(8,128)S(1)}, u32[]{:S(2)}, u32[]{:S(2)}) %collective-permute-start.15) | collective-permute-done | bytes 304 | tf_op jit(solution)/shard_map/ppermute | solution.py:26
  147.7 1.9 collective-permute-start.10
  149.6 2.4 collective-permute-start.11
  152.0 4.0 %collective-permute-done.11 = f32[3,34,1]{2,1,0:T(8,128)S(1)} collective-permute-done((f32[3,34,1]{2,1,0:T(8,128)S(1)}, f32[3,34,1]{2,1,0:T(8,128)S(1)}, u32[]{:S(2)}, u32[]{:S(2)}) %collective-permute-start.11) | collective-permute-done | bytes 440 | tf_op jit(solution)/shard_map/ppermute | solution.py:26
  156.6 23.2 %all-gather.3.cloned.1.call-done = f32[192,2,2048]{2,1,0:T(2,128)} async-done(((f32[6,2,2048]{2,1,0:T(2,128)}), f32[192,2,2048]{2,1,0:T(2,128)}) %all-gather.3.cloned.1.call-update) | async-done | bytes 3145744 | tf_op jit(solution)/shard_map/all_gather | solution.py:132
  179.8 3.4 %reduce_sum.9 = f32[6,2,2048]{2,1,0:T(2,128)S(1)} reduce(f32[32,6,2,2048]{3,2,1,0:T(2,128)} %bitcast.286, f32[]{:T(128)} %constant.138.clone.1), dimensions={0}, to_apply=%region_0.2 | reduce | flops 761856 | bytes 3244036 | tf_op jit(solution)/shard_map/reduce_sum | solution.py:132
  183.4 3.0 %collective-permute-start.16 = (f32[3,1,256]{2,1,0:T(1,128)S(1)}, f32[3,1,256]{2,1,0:T(1,128)S(1)}, u32[]{:S(2)}, u32[]{:S(2)}) collective-permute-start(f32[3,1,256]{2,1,0:T(1,128)S(1)} %get-tuple-element.78), channel_id=1, source_target_pairs={{0,8},{8,16},{16,24},{1,9},{9,17},{17,25},{2,10},{10,18},{18,26},{... | collective-permute-start | bytes 9224 | tf_op jit(solution)/shard_map/ppermute | solution.py:23
  186.4 1.3 collective-permute-start.17
  187.7 3.0 %collective-permute-done.17 = f32[3,1,256]{2,1,0:T(1,128)S(1)} collective-permute-done((f32[3,1,256]{2,1,0:T(1,128)S(1)}, f32[3,1,256]{2,1,0:T(1,128)S(1)}, u32[]{:S(2)}, u32[]{:S(2)}) %collective-permute-start.17) | collective-permute-done | bytes 3104 | tf_op jit(solution)/shard_map/ppermute | solution.py:26
  190.9 3.7 %collective-permute-start.18 = (f32[3,34,1]{2,1,0:T(8,128)S(1)}, f32[3,34,1]{2,1,0:T(8,128)S(1)}, u32[]{:S(2)}, u32[]{:S(2)}) collective-permute-start(f32[3,34,1]{2,1,0:T(8,128)S(1)} %get-tuple-element.64), channel_id=1, source_target_pairs={{0,1},{1,2},{2,3},{3,4},{4,5},{5,6},{6,7},{8,9},{9,10},{10,11},{11... | collective-permute-start | bytes 1232 | tf_op jit(solution)/shard_map/ppermute | solution.py:23
  194.6 1.9 collective-permute-start.19
  196.5 3.6 %collective-permute-done.19 = f32[3,34,1]{2,1,0:T(8,128)S(1)} collective-permute-done((f32[3,34,1]{2,1,0:T(8,128)S(1)}, f32[3,34,1]{2,1,0:T(8,128)S(1)}, u32[]{:S(2)}, u32[]{:S(2)}) %collective-permute-start.19) | collective-permute-done | bytes 440 | tf_op jit(solution)/shard_map/ppermute | solution.py:26
  200.8 4.0 %collective-permute-start.20 = (f32[3,1,256]{2,1,0:T(1,128)S(1)}, f32[3,1,256]{2,1,0:T(1,128)S(1)}, u32[]{:S(2)}, u32[]{:S(2)}) collective-permute-start(f32[3,1,256]{2,1,0:T(1,128)S(1)} %get-tuple-element.76), channel_id=1, source_target_pairs={{0,8},{8,16},{16,24},{1,9},{9,17},{17,25},{2,10},{10,18},{18,26},{... | collective-permute-start | bytes 9224 | tf_op jit(solution)/shard_map/ppermute | solution.py:23
  204.9 1.3 collective-permute-start.21
  206.2 3.0 %collective-permute-done.21 = f32[3,1,256]{2,1,0:T(1,128)S(1)} collective-permute-done((f32[3,1,256]{2,1,0:T(1,128)S(1)}, f32[3,1,256]{2,1,0:T(1,128)S(1)}, u32[]{:S(2)}, u32[]{:S(2)}) %collective-permute-start.21) | collective-permute-done | bytes 3104 | tf_op jit(solution)/shard_map/ppermute | solution.py:26
  209.3 3.3 %collective-permute-start.22 = (f32[3,34,1]{2,1,0:T(8,128)S(1)}, f32[3,34,1]{2,1,0:T(8,128)S(1)}, u32[]{:S(2)}, u32[]{:S(2)}) collective-permute-start(f32[3,34,1]{2,1,0:T(8,128)S(1)} %get-tuple-element.62), channel_id=1, source_target_pairs={{0,1},{1,2},{2,3},{3,4},{4,5},{5,6},{6,7},{8,9},{9,10},{10,11},{11... | collective-permute-start | bytes 1232 | tf_op jit(solution)/shard_map/ppermute | solution.py:23
  212.6 1.9 collective-permute-start.23
  214.6 3.6 %collective-permute-done.23 = f32[3,34,1]{2,1,0:T(8,128)S(1)} collective-permute-done((f32[3,34,1]{2,1,0:T(8,128)S(1)}, f32[3,34,1]{2,1,0:T(8,128)S(1)}, u32[]{:S(2)}, u32[]{:S(2)}) %collective-permute-start.23) | collective-permute-done | bytes 440 | tf_op jit(solution)/shard_map/ppermute | solution.py:26
  218.8 2.5 collective-permute-start.24
  221.4 1.3 collective-permute-start.25
  222.7 3.0 %collective-permute-done.25 = f32[3,1,256]{2,1,0:T(1,128)S(1)} collective-permute-done((f32[3,1,256]{2,1,0:T(1,128)S(1)}, f32[3,1,256]{2,1,0:T(1,128)S(1)}, u32[]{:S(2)}, u32[]{:S(2)}) %collective-permute-start.25) | collective-permute-done | bytes 3104 | tf_op jit(solution)/shard_map/ppermute | solution.py:26
  225.8 3.3 %collective-permute-start.26 = (f32[3,34,1]{2,1,0:T(8,128)S(1)}, f32[3,34,1]{2,1,0:T(8,128)S(1)}, u32[]{:S(2)}, u32[]{:S(2)}) collective-permute-start(f32[3,34,1]{2,1,0:T(8,128)S(1)} %get-tuple-element.60), channel_id=1, source_target_pairs={{0,1},{1,2},{2,3},{3,4},{4,5},{5,6},{6,7},{8,9},{9,10},{10,11},{11... | collective-permute-start | bytes 1232 | tf_op jit(solution)/shard_map/ppermute | solution.py:23
  229.1 1.9 collective-permute-start.27
  231.1 3.6 %collective-permute-done.27 = f32[3,34,1]{2,1,0:T(8,128)S(1)} collective-permute-done((f32[3,34,1]{2,1,0:T(8,128)S(1)}, f32[3,34,1]{2,1,0:T(8,128)S(1)}, u32[]{:S(2)}, u32[]{:S(2)}) %collective-permute-start.27) | collective-permute-done | bytes 440 | tf_op jit(solution)/shard_map/ppermute | solution.py:26
  235.4 2.5 collective-permute-start.28
  237.9 1.3 collective-permute-start.29
  239.2 3.0 %collective-permute-done.29 = f32[3,1,256]{2,1,0:T(1,128)S(1)} collective-permute-done((f32[3,1,256]{2,1,0:T(1,128)S(1)}, f32[3,1,256]{2,1,0:T(1,128)S(1)}, u32[]{:S(2)}, u32[]{:S(2)}) %collective-permute-start.29) | collective-permute-done | bytes 3104 | tf_op jit(solution)/shard_map/ppermute | solution.py:26
  242.4 3.3 %collective-permute-start.30 = (f32[3,34,1]{2,1,0:T(8,128)S(1)}, f32[3,34,1]{2,1,0:T(8,128)S(1)}, u32[]{:S(2)}, u32[]{:S(2)}) collective-permute-start(f32[3,34,1]{2,1,0:T(8,128)S(1)} %get-tuple-element.58), channel_id=1, source_target_pairs={{0,1},{1,2},{2,3},{3,4},{4,5},{5,6},{6,7},{8,9},{9,10},{10,11},{11... | collective-permute-start | bytes 1232 | tf_op jit(solution)/shard_map/ppermute | solution.py:23
  245.7 1.9 collective-permute-start.31
  247.6 3.6 %collective-permute-done.31 = f32[3,34,1]{2,1,0:T(8,128)S(1)} collective-permute-done((f32[3,34,1]{2,1,0:T(8,128)S(1)}, f32[3,34,1]{2,1,0:T(8,128)S(1)}, u32[]{:S(2)}, u32[]{:S(2)}) %collective-permute-start.31) | collective-permute-done | bytes 440 | tf_op jit(solution)/shard_map/ppermute | solution.py:26
  251.9 2.5 collective-permute-start.32
  254.5 1.3 collective-permute-start.33
  255.8 3.0 %collective-permute-done.33 = f32[3,1,256]{2,1,0:T(1,128)S(1)} collective-permute-done((f32[3,1,256]{2,1,0:T(1,128)S(1)}, f32[3,1,256]{2,1,0:T(1,128)S(1)}, u32[]{:S(2)}, u32[]{:S(2)}) %collective-permute-start.33) | collective-permute-done | bytes 3104 | tf_op jit(solution)/shard_map/ppermute | solution.py:26
  258.9 3.3 %collective-permute-start.34 = (f32[3,34,1]{2,1,0:T(8,128)S(1)}, f32[3,34,1]{2,1,0:T(8,128)S(1)}, u32[]{:S(2)}, u32[]{:S(2)}) collective-permute-start(f32[3,34,1]{2,1,0:T(8,128)S(1)} %get-tuple-element.56), channel_id=1, source_target_pairs={{0,1},{1,2},{2,3},{3,4},{4,5},{5,6},{6,7},{8,9},{9,10},{10,11},{11... | collective-permute-start | bytes 1232 | tf_op jit(solution)/shard_map/ppermute | solution.py:23
  262.2 1.9 collective-permute-start.35
  264.1 3.6 %collective-permute-done.35 = f32[3,34,1]{2,1,0:T(8,128)S(1)} collective-permute-done((f32[3,34,1]{2,1,0:T(8,128)S(1)}, f32[3,34,1]{2,1,0:T(8,128)S(1)}, u32[]{:S(2)}, u32[]{:S(2)}) %collective-permute-start.35) | collective-permute-done | bytes 440 | tf_op jit(solution)/shard_map/ppermute | solution.py:26
  (151 shorter events, 10.6 us)
Async XLA Ops:
  7.2 24.5 %copy-start = (f32[128,256]{1,0:T(8,128)S(1)}, f32[128,256]{1,0:T(8,128)}, u32[]{:S(2)}) copy-start(f32[128,256]{1,0:T(8,128)} %param.11) | copy-start | bytes 393220
  7.2 24.5 %copy-start.1 = (f32[2,128,256]{2,1,0:T(8,128)S(1)}, f32[2,128,256]{2,1,0:T(8,128)}, u32[]{:S(2)}) copy-start(f32[2,128,256]{2,1,0:T(8,128)} %param.12) | copy-start | bytes 786436
  7.2 172.6 %all-gather.3.cloned.1.call-start = ((), (), s32[]{:S(2)}) async-start(), calls=%async_computation | async-start | bytes 3244032 | tf_op jit(solution)/shard_map/all_gather | solution.py:132
  9.1 5.2 %collective-permute-start = (f32[4,1,256]{2,1,0:T(1,128)S(1)}, f32[4,1,256]{2,1,0:T(1,128)S(1)}, u32[]{:S(2)}, u32[]{:S(2)}) collective-permute-start(f32[4,1,256]{2,1,0:T(1,128)S(1)} %get-tuple-element.32), channel_id=1, source_target_pairs={{0,8},{8,16},{16,24},{1,9},{9,17},{17,25},{2,10},{10,18},{18,26},{... | collective-permute-start | bytes 12296 | tf_op jit(solution)/shard_map/ppermute | solution.py:23
  13.1 4.4 %collective-permute-start.1 = (f32[4,1,256]{2,1,0:T(1,128)S(1)}, f32[4,1,256]{2,1,0:T(1,128)S(1)}, u32[]{:S(2)}, u32[]{:S(2)}) collective-permute-start(f32[4,1,256]{2,1,0:T(1,128)S(1)} %get-tuple-element.33), channel_id=1, source_target_pairs={{8,0},{16,8},{24,16},{9,1},{17,9},{25,17},{10,2},{18,10},{26,18},{... | collective-permute-start | bytes 12296 | tf_op jit(solution)/shard_map/ppermute | solution.py:26
  18.4 14.2 %copy-start.2 = (f32[128,256]{1,0:T(8,128)S(1)}, f32[128,256]{1,0:T(8,128)}, u32[]{:S(2)}) copy-start(f32[128,256]{1,0:T(8,128)} %param.13) | copy-start | bytes 393220
  18.6 8.7 %collective-permute-start.2 = (f32[4,130,1]{2,1,0:T(8,128)S(1)}, f32[4,130,1]{2,1,0:T(8,128)S(1)}, u32[]{:S(2)}, u32[]{:S(2)}) collective-permute-start(f32[4,130,1]{2,1,0:T(8,128)S(1)} %get-tuple-element.28), channel_id=1, source_target_pairs={{0,1},{1,2},{2,3},{3,4},{4,5},{5,6},{6,7},{8,9},{9,10},{10,11},{11... | collective-permute-start | bytes 6248 | tf_op jit(solution)/shard_map/ppermute | solution.py:23
  23.8 7.9 %collective-permute-start.3 = (f32[4,130,1]{2,1,0:T(8,128)S(1)}, f32[4,130,1]{2,1,0:T(8,128)S(1)}, u32[]{:S(2)}, u32[]{:S(2)}) collective-permute-start(f32[4,130,1]{2,1,0:T(8,128)S(1)} %get-tuple-element.29), channel_id=1, source_target_pairs={{1,0},{2,1},{3,2},{4,3},{5,4},{6,5},{7,6},{9,8},{10,9},{11,10},{12... | collective-permute-start | bytes 6248 | tf_op jit(solution)/shard_map/ppermute | solution.py:26
  32.1 14.4 %copy-start.10 = (s32[2048]{0:T(1024)S(1)}, s32[2048]{0:T(1024)}, u32[]{:S(2)}) copy-start(s32[2048]{0:T(1024)} %param.19) | copy-start | bytes 24580
  32.8 5.3 %collective-permute-start.4 = (f32[4,1,256]{2,1,0:T(1,128)S(1)}, f32[4,1,256]{2,1,0:T(1,128)S(1)}, u32[]{:S(2)}, u32[]{:S(2)}) collective-permute-start(f32[4,1,256]{2,1,0:T(1,128)S(1)} %get-tuple-element.30), channel_id=1, source_target_pairs={{0,8},{8,16},{16,24},{1,9},{9,17},{17,25},{2,10},{10,18},{18,26},{... | collective-permute-start | bytes 12296 | tf_op jit(solution)/shard_map/ppermute | solution.py:23
  36.8 4.4 %collective-permute-start.5 = (f32[4,1,256]{2,1,0:T(1,128)S(1)}, f32[4,1,256]{2,1,0:T(1,128)S(1)}, u32[]{:S(2)}, u32[]{:S(2)}) collective-permute-start(f32[4,1,256]{2,1,0:T(1,128)S(1)} %get-tuple-element.31), channel_id=1, source_target_pairs={{8,0},{16,8},{24,16},{9,1},{17,9},{25,17},{10,2},{18,10},{26,18},{... | collective-permute-start | bytes 12296 | tf_op jit(solution)/shard_map/ppermute | solution.py:26
  41.4 52.6 %collective-permute-start.6 = (f32[4,130,1]{2,1,0:T(8,128)S(1)}, f32[4,130,1]{2,1,0:T(8,128)S(1)}, u32[]{:S(2)}, u32[]{:S(2)}) collective-permute-start(f32[4,130,1]{2,1,0:T(8,128)S(1)} %get-tuple-element.26), channel_id=1, source_target_pairs={{0,1},{1,2},{2,3},{3,4},{4,5},{5,6},{6,7},{8,9},{9,10},{10,11},{11... | collective-permute-start | bytes 6248 | tf_op jit(solution)/shard_map/ppermute | solution.py:23
  44.6 49.5 %collective-permute-start.7 = (f32[4,130,1]{2,1,0:T(8,128)S(1)}, f32[4,130,1]{2,1,0:T(8,128)S(1)}, u32[]{:S(2)}, u32[]{:S(2)}) collective-permute-start(f32[4,130,1]{2,1,0:T(8,128)S(1)} %get-tuple-element.27), channel_id=1, source_target_pairs={{1,0},{2,1},{3,2},{4,3},{5,4},{6,5},{7,6},{9,8},{10,9},{11,10},{12... | collective-permute-start | bytes 6248 | tf_op jit(solution)/shard_map/ppermute | solution.py:26
  95.1 11.9 %copy-start.3 = (f32[128,256]{1,0:T(8,128)}, f32[128,256]{1,0:T(8,128)S(1)}, u32[]{:S(2)}) copy-start(f32[128,256]{1,0:T(8,128)S(1)} %get-tuple-element.7) | copy-start | bytes 393220
  107.1 12.8 %copy-start.6 = (f32[11]{0:T(128)S(1)}, f32[11]{0:T(128)}, u32[]{:S(2)}) copy-start(f32[11]{0:T(128)} %param.18) | copy-start | bytes 136
  107.1 13.5 %copy-start.9 = (s32[32,256]{1,0:T(8,128)S(1)}, s32[32,256]{1,0:T(8,128)}, u32[]{:S(2)}) copy-start(s32[32,256]{1,0:T(8,128)} %param.17) | copy-start | bytes 98308
  107.1 20.6 %copy-start.4 = (f32[32,256]{1,0:T(8,128)S(1)}, f32[32,256]{1,0:T(8,128)}, u32[]{:S(2)}) copy-start(f32[32,256]{1,0:T(8,128)} %param.14) | copy-start | bytes 98308
  107.1 25.0 %copy-start.7 = (f32[32,256]{1,0:T(8,128)S(1)}, f32[32,256]{1,0:T(8,128)}, u32[]{:S(2)}) copy-start(f32[32,256]{1,0:T(8,128)} %param.15) | copy-start | bytes 98308
  107.1 25.0 %copy-start.8 = (s32[32,256]{1,0:T(8,128)S(1)}, s32[32,256]{1,0:T(8,128)}, u32[]{:S(2)}) copy-start(s32[32,256]{1,0:T(8,128)} %param.16) | copy-start | bytes 98308
  119.3 0.6 copy-start.5
  127.7 9.8 %collective-permute-start.12 = (f32[2,1,256]{2,1,0:T(1,128)S(1)}, f32[2,1,256]{2,1,0:T(1,128)S(1)}, u32[]{:S(2)}, u32[]{:S(2)}) collective-permute-start(f32[2,1,256]{2,1,0:T(1,128)S(1)} %get-tuple-element.82), channel_id=1, source_target_pairs={{0,8},{8,16},{16,24},{1,9},{9,17},{17,25},{2,10},{10,18},{18,26},{... | collective-permute-start | bytes 6152 | tf_op jit(solution)/shard_map/ppermute | solution.py:23
  130.8 6.7 %collective-permute-start.13 = (f32[2,1,256]{2,1,0:T(1,128)S(1)}, f32[2,1,256]{2,1,0:T(1,128)S(1)}, u32[]{:S(2)}, u32[]{:S(2)}) collective-permute-start(f32[2,1,256]{2,1,0:T(1,128)S(1)} %get-tuple-element.83), channel_id=1, source_target_pairs={{8,0},{16,8},{24,16},{9,1},{17,9},{25,17},{10,2},{18,10},{26,18},{... | collective-permute-start | bytes 6152 | tf_op jit(solution)/shard_map/ppermute | solution.py:26
  132.2 15.4 %collective-permute-start.8 = (f32[3,1,256]{2,1,0:T(1,128)S(1)}, f32[3,1,256]{2,1,0:T(1,128)S(1)}, u32[]{:S(2)}, u32[]{:S(2)}) collective-permute-start(f32[3,1,256]{2,1,0:T(1,128)S(1)} %get-tuple-element.108), channel_id=1, source_target_pairs={{0,8},{8,16},{16,24},{1,9},{9,17},{17,25},{2,10},{10,18},{18,26},{... | collective-permute-start | bytes 9224 | tf_op jit(solution)/shard_map/ppermute | solution.py:23
  136.1 11.4 %collective-permute-start.9 = (f32[3,1,256]{2,1,0:T(1,128)S(1)}, f32[3,1,256]{2,1,0:T(1,128)S(1)}, u32[]{:S(2)}, u32[]{:S(2)}) collective-permute-start(f32[3,1,256]{2,1,0:T(1,128)S(1)} %get-tuple-element.109), channel_id=1, source_target_pairs={{8,0},{16,8},{24,16},{9,1},{17,9},{25,17},{10,2},{18,10},{26,18},{... | collective-permute-start | bytes 9224 | tf_op jit(solution)/shard_map/ppermute | solution.py:26
  137.6 6.4 %collective-permute-start.14 = (f32[2,34,1]{2,1,0:T(8,128)S(1)}, f32[2,34,1]{2,1,0:T(8,128)S(1)}, u32[]{:S(2)}, u32[]{:S(2)}) collective-permute-start(f32[2,34,1]{2,1,0:T(8,128)S(1)} %get-tuple-element.80), channel_id=1, source_target_pairs={{0,1},{1,2},{2,3},{3,4},{4,5},{5,6},{6,7},{8,9},{9,10},{10,11},{11... | collective-permute-start | bytes 824 | tf_op jit(solution)/shard_map/ppermute | solution.py:23
  142.1 5.3 %collective-permute-start.15 = (f32[2,34,1]{2,1,0:T(8,128)S(1)}, f32[2,34,1]{2,1,0:T(8,128)S(1)}, u32[]{:S(2)}, u32[]{:S(2)}) collective-permute-start(f32[2,34,1]{2,1,0:T(8,128)S(1)} %get-tuple-element.81), channel_id=1, source_target_pairs={{1,0},{2,1},{3,2},{4,3},{5,4},{6,5},{7,6},{9,8},{10,9},{11,10},{12... | collective-permute-start | bytes 824 | tf_op jit(solution)/shard_map/ppermute | solution.py:26
  147.7 4.4 %collective-permute-start.10 = (f32[3,34,1]{2,1,0:T(8,128)S(1)}, f32[3,34,1]{2,1,0:T(8,128)S(1)}, u32[]{:S(2)}, u32[]{:S(2)}) collective-permute-start(f32[3,34,1]{2,1,0:T(8,128)S(1)} %get-tuple-element.68), channel_id=1, source_target_pairs={{0,1},{1,2},{2,3},{3,4},{4,5},{5,6},{6,7},{8,9},{9,10},{10,11},{11... | collective-permute-start | bytes 1232 | tf_op jit(solution)/shard_map/ppermute | solution.py:23
  149.6 6.5 %collective-permute-start.11 = (f32[3,34,1]{2,1,0:T(8,128)S(1)}, f32[3,34,1]{2,1,0:T(8,128)S(1)}, u32[]{:S(2)}, u32[]{:S(2)}) collective-permute-start(f32[3,34,1]{2,1,0:T(8,128)S(1)} %get-tuple-element.69), channel_id=1, source_target_pairs={{1,0},{2,1},{3,2},{4,3},{5,4},{6,5},{7,6},{9,8},{10,9},{11,10},{12... | collective-permute-start | bytes 1232 | tf_op jit(solution)/shard_map/ppermute | solution.py:26
  183.4 4.4 %collective-permute-start.16 = (f32[3,1,256]{2,1,0:T(1,128)S(1)}, f32[3,1,256]{2,1,0:T(1,128)S(1)}, u32[]{:S(2)}, u32[]{:S(2)}) collective-permute-start(f32[3,1,256]{2,1,0:T(1,128)S(1)} %get-tuple-element.78), channel_id=1, source_target_pairs={{0,8},{8,16},{16,24},{1,9},{9,17},{17,25},{2,10},{10,18},{18,26},{... | collective-permute-start | bytes 9224 | tf_op jit(solution)/shard_map/ppermute | solution.py:23
  186.4 4.3 %collective-permute-start.17 = (f32[3,1,256]{2,1,0:T(1,128)S(1)}, f32[3,1,256]{2,1,0:T(1,128)S(1)}, u32[]{:S(2)}, u32[]{:S(2)}) collective-permute-start(f32[3,1,256]{2,1,0:T(1,128)S(1)} %get-tuple-element.79), channel_id=1, source_target_pairs={{8,0},{16,8},{24,16},{9,1},{17,9},{25,17},{10,2},{18,10},{26,18},{... | collective-permute-start | bytes 9224 | tf_op jit(solution)/shard_map/ppermute | solution.py:26
  190.9 5.6 %collective-permute-start.18 = (f32[3,34,1]{2,1,0:T(8,128)S(1)}, f32[3,34,1]{2,1,0:T(8,128)S(1)}, u32[]{:S(2)}, u32[]{:S(2)}) collective-permute-start(f32[3,34,1]{2,1,0:T(8,128)S(1)} %get-tuple-element.64), channel_id=1, source_target_pairs={{0,1},{1,2},{2,3},{3,4},{4,5},{5,6},{6,7},{8,9},{9,10},{10,11},{11... | collective-permute-start | bytes 1232 | tf_op jit(solution)/shard_map/ppermute | solution.py:23
  194.6 5.5 %collective-permute-start.19 = (f32[3,34,1]{2,1,0:T(8,128)S(1)}, f32[3,34,1]{2,1,0:T(8,128)S(1)}, u32[]{:S(2)}, u32[]{:S(2)}) collective-permute-start(f32[3,34,1]{2,1,0:T(8,128)S(1)} %get-tuple-element.65), channel_id=1, source_target_pairs={{1,0},{2,1},{3,2},{4,3},{5,4},{6,5},{7,6},{9,8},{10,9},{11,10},{12... | collective-permute-start | bytes 1232 | tf_op jit(solution)/shard_map/ppermute | solution.py:26
  200.8 5.4 %collective-permute-start.20 = (f32[3,1,256]{2,1,0:T(1,128)S(1)}, f32[3,1,256]{2,1,0:T(1,128)S(1)}, u32[]{:S(2)}, u32[]{:S(2)}) collective-permute-start(f32[3,1,256]{2,1,0:T(1,128)S(1)} %get-tuple-element.76), channel_id=1, source_target_pairs={{0,8},{8,16},{16,24},{1,9},{9,17},{17,25},{2,10},{10,18},{18,26},{... | collective-permute-start | bytes 9224 | tf_op jit(solution)/shard_map/ppermute | solution.py:23
  204.9 4.3 %collective-permute-start.21 = (f32[3,1,256]{2,1,0:T(1,128)S(1)}, f32[3,1,256]{2,1,0:T(1,128)S(1)}, u32[]{:S(2)}, u32[]{:S(2)}) collective-permute-start(f32[3,1,256]{2,1,0:T(1,128)S(1)} %get-tuple-element.77), channel_id=1, source_target_pairs={{8,0},{16,8},{24,16},{9,1},{17,9},{25,17},{10,2},{18,10},{26,18},{... | collective-permute-start | bytes 9224 | tf_op jit(solution)/shard_map/ppermute | solution.py:26
  209.3 5.2 %collective-permute-start.22 = (f32[3,34,1]{2,1,0:T(8,128)S(1)}, f32[3,34,1]{2,1,0:T(8,128)S(1)}, u32[]{:S(2)}, u32[]{:S(2)}) collective-permute-start(f32[3,34,1]{2,1,0:T(8,128)S(1)} %get-tuple-element.62), channel_id=1, source_target_pairs={{0,1},{1,2},{2,3},{3,4},{4,5},{5,6},{6,7},{8,9},{9,10},{10,11},{11... | collective-permute-start | bytes 1232 | tf_op jit(solution)/shard_map/ppermute | solution.py:23
  212.6 5.5 %collective-permute-start.23 = (f32[3,34,1]{2,1,0:T(8,128)S(1)}, f32[3,34,1]{2,1,0:T(8,128)S(1)}, u32[]{:S(2)}, u32[]{:S(2)}) collective-permute-start(f32[3,34,1]{2,1,0:T(8,128)S(1)} %get-tuple-element.63), channel_id=1, source_target_pairs={{1,0},{2,1},{3,2},{4,3},{5,4},{6,5},{7,6},{9,8},{10,9},{11,10},{12... | collective-permute-start | bytes 1232 | tf_op jit(solution)/shard_map/ppermute | solution.py:26
  218.8 3.9 %collective-permute-start.24 = (f32[3,1,256]{2,1,0:T(1,128)S(1)}, f32[3,1,256]{2,1,0:T(1,128)S(1)}, u32[]{:S(2)}, u32[]{:S(2)}) collective-permute-start(f32[3,1,256]{2,1,0:T(1,128)S(1)} %get-tuple-element.74), channel_id=1, source_target_pairs={{0,8},{8,16},{16,24},{1,9},{9,17},{17,25},{2,10},{10,18},{18,26},{... | collective-permute-start | bytes 9224 | tf_op jit(solution)/shard_map/ppermute | solution.py:23
  221.4 4.3 %collective-permute-start.25 = (f32[3,1,256]{2,1,0:T(1,128)S(1)}, f32[3,1,256]{2,1,0:T(1,128)S(1)}, u32[]{:S(2)}, u32[]{:S(2)}) collective-permute-start(f32[3,1,256]{2,1,0:T(1,128)S(1)} %get-tuple-element.75), channel_id=1, source_target_pairs={{8,0},{16,8},{24,16},{9,1},{17,9},{25,17},{10,2},{18,10},{26,18},{... | collective-permute-start | bytes 9224 | tf_op jit(solution)/shard_map/ppermute | solution.py:26
  225.8 5.2 %collective-permute-start.26 = (f32[3,34,1]{2,1,0:T(8,128)S(1)}, f32[3,34,1]{2,1,0:T(8,128)S(1)}, u32[]{:S(2)}, u32[]{:S(2)}) collective-permute-start(f32[3,34,1]{2,1,0:T(8,128)S(1)} %get-tuple-element.60), channel_id=1, source_target_pairs={{0,1},{1,2},{2,3},{3,4},{4,5},{5,6},{6,7},{8,9},{9,10},{10,11},{11... | collective-permute-start | bytes 1232 | tf_op jit(solution)/shard_map/ppermute | solution.py:23
  229.1 5.5 %collective-permute-start.27 = (f32[3,34,1]{2,1,0:T(8,128)S(1)}, f32[3,34,1]{2,1,0:T(8,128)S(1)}, u32[]{:S(2)}, u32[]{:S(2)}) collective-permute-start(f32[3,34,1]{2,1,0:T(8,128)S(1)} %get-tuple-element.61), channel_id=1, source_target_pairs={{1,0},{2,1},{3,2},{4,3},{5,4},{6,5},{7,6},{9,8},{10,9},{11,10},{12... | collective-permute-start | bytes 1232 | tf_op jit(solution)/shard_map/ppermute | solution.py:26
  235.4 3.9 %collective-permute-start.28 = (f32[3,1,256]{2,1,0:T(1,128)S(1)}, f32[3,1,256]{2,1,0:T(1,128)S(1)}, u32[]{:S(2)}, u32[]{:S(2)}) collective-permute-start(f32[3,1,256]{2,1,0:T(1,128)S(1)} %get-tuple-element.72), channel_id=1, source_target_pairs={{0,8},{8,16},{16,24},{1,9},{9,17},{17,25},{2,10},{10,18},{18,26},{... | collective-permute-start | bytes 9224 | tf_op jit(solution)/shard_map/ppermute | solution.py:23
  237.9 4.3 %collective-permute-start.29 = (f32[3,1,256]{2,1,0:T(1,128)S(1)}, f32[3,1,256]{2,1,0:T(1,128)S(1)}, u32[]{:S(2)}, u32[]{:S(2)}) collective-permute-start(f32[3,1,256]{2,1,0:T(1,128)S(1)} %get-tuple-element.73), channel_id=1, source_target_pairs={{8,0},{16,8},{24,16},{9,1},{17,9},{25,17},{10,2},{18,10},{26,18},{... | collective-permute-start | bytes 9224 | tf_op jit(solution)/shard_map/ppermute | solution.py:26
  242.4 5.2 %collective-permute-start.30 = (f32[3,34,1]{2,1,0:T(8,128)S(1)}, f32[3,34,1]{2,1,0:T(8,128)S(1)}, u32[]{:S(2)}, u32[]{:S(2)}) collective-permute-start(f32[3,34,1]{2,1,0:T(8,128)S(1)} %get-tuple-element.58), channel_id=1, source_target_pairs={{0,1},{1,2},{2,3},{3,4},{4,5},{5,6},{6,7},{8,9},{9,10},{10,11},{11... | collective-permute-start | bytes 1232 | tf_op jit(solution)/shard_map/ppermute | solution.py:23
  245.7 5.5 %collective-permute-start.31 = (f32[3,34,1]{2,1,0:T(8,128)S(1)}, f32[3,34,1]{2,1,0:T(8,128)S(1)}, u32[]{:S(2)}, u32[]{:S(2)}) collective-permute-start(f32[3,34,1]{2,1,0:T(8,128)S(1)} %get-tuple-element.59), channel_id=1, source_target_pairs={{1,0},{2,1},{3,2},{4,3},{5,4},{6,5},{7,6},{9,8},{10,9},{11,10},{12... | collective-permute-start | bytes 1232 | tf_op jit(solution)/shard_map/ppermute | solution.py:26
  251.9 3.9 %collective-permute-start.32 = (f32[3,1,256]{2,1,0:T(1,128)S(1)}, f32[3,1,256]{2,1,0:T(1,128)S(1)}, u32[]{:S(2)}, u32[]{:S(2)}) collective-permute-start(f32[3,1,256]{2,1,0:T(1,128)S(1)} %get-tuple-element.70), channel_id=1, source_target_pairs={{0,8},{8,16},{16,24},{1,9},{9,17},{17,25},{2,10},{10,18},{18,26},{... | collective-permute-start | bytes 9224 | tf_op jit(solution)/shard_map/ppermute | solution.py:23
  254.5 4.3 %collective-permute-start.33 = (f32[3,1,256]{2,1,0:T(1,128)S(1)}, f32[3,1,256]{2,1,0:T(1,128)S(1)}, u32[]{:S(2)}, u32[]{:S(2)}) collective-permute-start(f32[3,1,256]{2,1,0:T(1,128)S(1)} %get-tuple-element.71), channel_id=1, source_target_pairs={{8,0},{16,8},{24,16},{9,1},{17,9},{25,17},{10,2},{18,10},{26,18},{... | collective-permute-start | bytes 9224 | tf_op jit(solution)/shard_map/ppermute | solution.py:26
  258.9 5.2 %collective-permute-start.34 = (f32[3,34,1]{2,1,0:T(8,128)S(1)}, f32[3,34,1]{2,1,0:T(8,128)S(1)}, u32[]{:S(2)}, u32[]{:S(2)}) collective-permute-start(f32[3,34,1]{2,1,0:T(8,128)S(1)} %get-tuple-element.56), channel_id=1, source_target_pairs={{0,1},{1,2},{2,3},{3,4},{4,5},{5,6},{6,7},{8,9},{9,10},{10,11},{11... | collective-permute-start | bytes 1232 | tf_op jit(solution)/shard_map/ppermute | solution.py:23
  262.2 5.5 %collective-permute-start.35 = (f32[3,34,1]{2,1,0:T(8,128)S(1)}, f32[3,34,1]{2,1,0:T(8,128)S(1)}, u32[]{:S(2)}, u32[]{:S(2)}) collective-permute-start(f32[3,34,1]{2,1,0:T(8,128)S(1)} %get-tuple-element.57), channel_id=1, source_target_pairs={{1,0},{2,1},{3,2},{4,3},{5,4},{6,5},{7,6},{9,8},{10,9},{11,10},{12... | collective-permute-start | bytes 1232 | tf_op jit(solution)/shard_map/ppermute | solution.py:26
Sparse Core Ops, SparseCore 0:
  120.0 59.7 all-gather.2
